TPU v7x, 32 devices: a whole 2x2x4 slice. The times are simulated.
32 devices in a mesh: grp: 4 (over y, x), dev: 8 (over z, core).
Axes of the slice: x: 2, y: 2, z: 4, core: 2. Of those that a mesh axis runs over, the one named last changes fastest.
Arguments:
- fine_nodes: bfloat16 [81920, 512], P(('grp', 'dev')), may hold values from -6 to 6
- mid_nodes: bfloat16 [20480, 512], P(('grp', 'dev')), may hold values from -6 to 6
- coarse_nodes: bfloat16 [5120, 512], P('dev'), may hold values from -6 to 6
- fine_owner: int32 [81920, 1], P(('grp', 'dev')), may hold values from 0 to 31, as said below
- fine_parent: int32 [81920], P(('grp', 'dev')), may hold values from 0 to 639
- mid_owner: int32 [20480, 1], P(('grp', 'dev')), may hold values from 0 to 7, as said below
- mid_parent: int32 [20480], P(('grp', 'dev')), may hold values from 0 to 639
- neighbours: int32 [5120, 6], P('dev'), may hold values from 0 to 5119, as said below
- neighbour_mask: int32 [5120, 6], P('dev'), may hold values from 0 to 1, as said below
- up_child_w: bfloat16 [512, 512], replicated, may hold values from -0.25 to 0.25
- up_parent_w: bfloat16 [512, 512], replicated, may hold values from -0.25 to 0.25
- up_out_w: bfloat16 [512, 512], replicated, may hold values from -0.25 to 0.25
- up_bias: float32 [512], replicated, may hold values from -3 to 3
- up_gain: float32 [512], replicated, may hold values from 0.1 to 1.9
- mid_child_w: bfloat16 [512, 512], replicated, may hold values from -0.25 to 0.25
- mid_parent_w: bfloat16 [512, 512], replicated, may hold values from -0.25 to 0.25
- mid_out_w: bfloat16 [512, 512], replicated, may hold values from -0.25 to 0.25
- mid_bias: float32 [512], replicated, may hold values from -3 to 3
- mid_gain: float32 [512], replicated, may hold values from 0.1 to 1.9
- same_self_w: bfloat16 [512, 512], replicated, may hold values from -0.25 to 0.25
- same_other_w: bfloat16 [512, 512], replicated, may hold values from -0.25 to 0.25
- same_out_w: bfloat16 [512, 512], replicated, may hold values from -0.25 to 0.25
- same_bias: float32 [512], replicated, may hold values from -3 to 3
- same_gain: float32 [512], replicated, may hold values from 0.1 to 1.9
- down_child_w: bfloat16 [512, 512], replicated, may hold values from -0.25 to 0.25
- down_parent_w: bfloat16 [512, 512], replicated, may hold values from -0.25 to 0.25
- down_out_w: bfloat16 [512, 512], replicated, may hold values from -0.25 to 0.25
- down_bias: float32 [512], replicated, may hold values from -3 to 3
- down_gain: float32 [512], replicated, may hold values from 0.1 to 1.9
Outputs:
- mid_out: bfloat16 [20480, 512], P(('grp', 'dev'))
- coarse_out: bfloat16 [5120, 512], P('dev')
Inputs may be any that keep to these rules, and one draw needn't show every extreme that they name: `fine_owner`: each device's rows name that device itself or one of the four devices up to two places away along grp+dev, counted around the end. No device other than itself is named more than 320 times from one device's rows, and every device's rows name one of them exactly 320 times. `mid_owner`: the rows of the device at index d of dev name d or an index up to two places away from d along dev, counted around the end. No index other than d is named more than 80 times from one device's rows, and every device's rows name one of them exactly 80 times. `neighbours`: row i names rows within 640 places of i, counted around the end of the 5120 rows, never i itself. `neighbour_mask`: exactly 12 rows have one unused slot, the last one; all other slots are used.
All inputs are finite; a program needn't handle non-finite values.
Results may differ from a plain program's by a relative error of at most 0.01.
Values may be sent and summed in bfloat16 or wider, within the bound.
A program may use at most 128 MiB of HBM per device.

v0:
```python
import jax
import jax.numpy as jnp
from jax import lax
from jax.sharding import PartitionSpec as P


def from_behind(value, axis, steps):
    count = lax.axis_size(axis)
    pairs = [(source, (source + steps) % count) for source in range(count)]
    return lax.ppermute(value, axis, pairs)


def extended(block, sides, width):
    for axis, dim in sides:
        count = lax.axis_size(axis)
        forward = [(i, i + 1) for i in range(count - 1)]
        forward.append((count - 1, 0))
        backward = [(target, source) for source, target in forward]
        low = lax.ppermute(
            lax.slice_in_dim(block, block.shape[dim] - width, None, axis=dim), axis, forward
        )
        high = lax.ppermute(lax.slice_in_dim(block, 0, width, axis=dim), axis, backward)
        block = jnp.concatenate([low, block, high], axis=dim)
    return block


def layer_norm(values, gain):
    center = values - jnp.mean(values, axis=-1, keepdims=True)
    spread = jnp.mean(center * center, axis=-1, keepdims=True)
    return center * lax.rsqrt(spread + 1e-05) * gain


def spill_layout(owner, device_index, total, capacity):
    codes = jnp.array([total - 2, total - 1, 1, 2], jnp.int32)
    relative = (owner - device_index) % total
    choose = (relative[:, None] == codes[None, :]).astype(jnp.int32)
    before = jnp.cumsum(choose, axis=0) - choose
    placed = jnp.sum(before * choose, axis=1)
    column = jnp.sum(choose * jnp.arange(4, dtype=jnp.int32)[None, :], axis=1)
    spilled = jnp.sum(choose, axis=1) > 0
    position = jnp.where(spilled, column * capacity + placed, 4 * capacity)
    return (relative == 0, position)


def fill_slots(rows, parents, position, total):
    buffer = jnp.zeros((total, rows.shape[1]), rows.dtype).at[position].set(rows, mode="drop")
    labels = jnp.full((total,), -1, jnp.int32).at[position].set(parents, mode="drop")
    return (buffer, labels)


def receive_messages(rows, labels, parent_terms, w_child, w_out, bias):
    picked = jnp.take(parent_terms, jnp.maximum(labels, 0), axis=0)
    hidden = jax.nn.silu(jnp.dot(rows, w_child, preferred_element_type=jnp.float32) + picked + bias)
    message = jnp.dot(
        hidden.astype(jnp.bfloat16), w_out, preferred_element_type=jnp.float32
    ).astype(jnp.bfloat16)
    member = (
        labels[None, :] == jnp.arange(parent_terms.shape[0], dtype=jnp.int32)[:, None]
    ).astype(jnp.bfloat16)
    return jnp.dot(member, message, preferred_element_type=jnp.float32)


def on_device(
    fine_nodes,
    mid_nodes,
    coarse_nodes,
    fine_owner,
    fine_parent,
    mid_owner,
    mid_parent,
    neighbours,
    neighbour_mask,
    up_child_w,
    up_parent_w,
    up_out_w,
    up_bias,
    up_gain,
    mid_child_w,
    mid_parent_w,
    mid_out_w,
    mid_bias,
    mid_gain,
    same_self_w,
    same_other_w,
    same_out_w,
    same_bias,
    same_gain,
    down_child_w,
    down_parent_w,
    down_out_w,
    down_bias,
    down_gain,
):
    groups = lax.axis_size("grp")
    members = lax.axis_size("dev")
    everyone = groups * members
    fine_count = fine_nodes.shape[0]
    width = fine_nodes.shape[1]
    fine_capacity = fine_count // 8
    device_index = lax.axis_index("grp") * members + lax.axis_index("dev")
    own_fine, position = spill_layout(fine_owner[:, 0], device_index, everyone, fine_capacity)
    buffer, labels = fill_slots(fine_nodes, fine_parent, position, 4 * fine_capacity)
    fine_rows = [fine_nodes]
    fine_labels = [jnp.where(own_fine, fine_parent, -1)]
    for column, offset in enumerate((-2, -1, 1, 2)):
        lower = column * fine_capacity
        upper = lower + fine_capacity
        got_rows, got_labels = from_behind(
            (buffer[lower:upper], labels[lower:upper]), ("grp", "dev"), offset
        )
        fine_rows.append(got_rows)
        fine_labels.append(got_labels)
    mid_terms = jnp.dot(mid_nodes, up_parent_w, preferred_element_type=jnp.float32)
    fine_sum = receive_messages(
        jnp.concatenate(fine_rows, axis=0),
        jnp.concatenate(fine_labels, axis=0),
        mid_terms,
        up_child_w,
        up_out_w,
        up_bias,
    )
    mid_update = (mid_nodes.astype(jnp.float32) + layer_norm(fine_sum, up_gain)).astype(
        jnp.bfloat16
    )
    mid_count = mid_nodes.shape[0]
    coarse_count = coarse_nodes.shape[0]
    mid_capacity = mid_count // 8
    dev_index = lax.axis_index("dev")
    own_mid, mid_position = spill_layout(mid_owner[:, 0], dev_index, members, mid_capacity)
    mid_buffer, mid_labels = fill_slots(mid_update, mid_parent, mid_position, 4 * mid_capacity)
    mid_rows = [mid_update]
    mid_label_list = [jnp.where(own_mid, mid_parent, -1)]
    for column, offset in enumerate((-2, -1, 1, 2)):
        lower = column * mid_capacity
        upper = lower + mid_capacity
        got_rows, got_labels = from_behind(
            (mid_buffer[lower:upper], mid_labels[lower:upper]), "dev", offset
        )
        mid_rows.append(got_rows)
        mid_label_list.append(got_labels)
    coarse_terms = jnp.dot(coarse_nodes, mid_parent_w, preferred_element_type=jnp.float32)
    partial_sum = receive_messages(
        jnp.concatenate(mid_rows, axis=0),
        jnp.concatenate(mid_label_list, axis=0),
        coarse_terms,
        mid_child_w,
        mid_out_w,
        mid_bias,
    )
    coarse_sum = lax.psum(partial_sum.astype(jnp.bfloat16), "grp").astype(jnp.float32)
    row_count = coarse_nodes.shape[0]
    coarse_update = (coarse_nodes.astype(jnp.float32) + layer_norm(coarse_sum, mid_gain)).astype(
        jnp.bfloat16
    )
    self_terms = jnp.dot(coarse_update, same_self_w, preferred_element_type=jnp.float32)
    other_terms = jnp.dot(coarse_update, same_other_w, preferred_element_type=jnp.float32).astype(
        jnp.bfloat16
    )
    rim = extended(other_terms, (("dev", 0),), coarse_count)
    local = (neighbours - dev_index * coarse_count + coarse_count) % (members * coarse_count)
    slots = neighbours.shape[1]
    hidden_width = other_terms.shape[1]
    picked = jnp.take(rim, local.reshape(-1), axis=0).reshape(row_count, slots, hidden_width)
    same_hidden = jax.nn.silu(
        self_terms[:, None, :] + picked.astype(jnp.float32) + same_bias
    ).astype(jnp.bfloat16)
    message = jnp.dot(
        same_hidden.reshape(row_count * slots, hidden_width),
        same_out_w,
        preferred_element_type=jnp.float32,
    ).reshape(row_count, slots, width)
    same_sum = jnp.sum(message * neighbour_mask[:, :, None].astype(jnp.float32), axis=1)
    coarse_part = (coarse_update.astype(jnp.float32) + layer_norm(same_sum, same_gain)).astype(
        jnp.bfloat16
    )
    down_part = jnp.dot(coarse_part, down_parent_w, preferred_element_type=jnp.float32).astype(
        jnp.bfloat16
    )
    returned = [jnp.take(down_part, jnp.maximum(mid_parent, 0), axis=0)]
    for column, offset in enumerate((-2, -1, 1, 2)):
        outgoing = jnp.take(down_part, jnp.maximum(mid_label_list[column + 1], 0), axis=0)
        returned.append(from_behind(outgoing, "dev", -offset))
    stacked = jnp.concatenate(returned, axis=0)
    choose_row = jnp.where(
        own_mid, jnp.arange(mid_count, dtype=jnp.int32), mid_count + mid_position
    )
    parent_rows = jnp.take(stacked, choose_row, axis=0)
    down_hidden = jax.nn.silu(
        jnp.dot(mid_update, down_child_w, preferred_element_type=jnp.float32)
        + parent_rows.astype(jnp.float32)
        + down_bias
    )
    down_messages = jnp.dot(
        down_hidden.astype(jnp.bfloat16), down_out_w, preferred_element_type=jnp.float32
    )
    mid_out = (mid_update.astype(jnp.float32) + layer_norm(down_messages, down_gain)).astype(
        jnp.bfloat16
    )
    return (mid_out, coarse_part)


def solution(mesh):
    in_specs = (
        P(("grp", "dev"), None),
        P(("grp", "dev"), None),
        P("dev", None),
        P(("grp", "dev"), None),
        P(("grp", "dev")),
        P(("grp", "dev"), None),
        P(("grp", "dev")),
        P("dev", None),
        P("dev", None),
        P(),
        P(),
        P(),
        P(),
        P(),
        P(),
        P(),
        P(),
        P(),
        P(),
        P(),
        P(),
        P(),
        P(),
        P(),
        P(),
        P(),
        P(),
        P(),
        P(),
    )
    out_specs = (P(("grp", "dev"), None), P("dev", None))
    return jax.shard_map(
        on_device, mesh=mesh, in_specs=in_specs, out_specs=out_specs, check_vma=False
    )
```

profile of v0, /device:TPU:0, one launch (start us, length us, event | category | flops | bytes accessed | tf_op | source)
XLA Modules:
  0.0 269.7 jit_solution(285216280650305009)
XLA Ops:
  11.4 12.4 %scatter_custom_fusion.1 = bf16[1280,512]{1,0:T(8,128)(2,1)S(1)} fusion(s32[2560]{0:T(1024)S(1)} %fusion.37, bf16[2560,512]{1,0:T(8,128)(2,1)} %param.33, bf16[]{:T(256)} %constant.182.clone.1), kind=kCustom, calls=%fused_computation.57 | custom fusion | bytes 1311232 | tf_op jit(solution)/shard_map/scatter | solution.py:46
  24.8 6.9 %collective-permute-start.4 = (bf16[320,512]{1,0:T(8,128)(2,1)}, bf16[320,512]{1,0:T(8,128)(2,1)}, u32[]{:S(2)}, u32[]{:S(2)}) collective-permute-start(bf16[320,512]{1,0:T(8,128)(2,1)} %get-tuple-element.24), channel_id=1, source_target_pairs={{0,30},{1,31},{2,0},{3,1},{4,2},{5,3},{6,4},{7,5},{8,6},{9,7},{10,... | collective-permute-start | bytes 983048 | tf_op jit(solution)/shard_map/ppermute | solution.py:10
  31.7 9.9 %scatter_custom_fusion = s32[1280]{0:T(1024)S(1)} fusion(s32[2560]{0:T(1024)S(1)} %fusion.37, s32[2560]{0:T(1024)S(1)} %copy-done.20, s32[]{:T(128)} %constant.179.clone.1), kind=kCustom, calls=%fused_computation.152 | custom fusion | bytes 5124 | tf_op jit(solution)/shard_map/scatter | solution.py:47
  44.5 4.1 %scatter_custom_fusion.2 = s32[320]{0:T(512)S(1)} fusion(s32[640]{0:T(1024)S(1)} %fusion.46, s32[640]{0:T(1024)S(1)} %copy-done.19, s32[]{:T(128)} %constant.179.clone.1), kind=kCustom, calls=%fused_computation.165 | custom fusion | bytes 1284 | tf_op jit(solution)/shard_map/scatter | solution.py:47
  49.3 3.5 %constant_dynamic-update-slice_fusion.4 = bf16[3840,512]{1,0:T(8,128)(2,1)} fusion(bf16[2560,512]{1,0:T(8,128)(2,1)} %param.33), kind=kLoop, calls=%fused_computation.88 | loop fusion | bytes 5242880
  69.7 5.2 %collective-permute-start.5 = (bf16[320,512]{1,0:T(8,128)(2,1)}, bf16[320,512]{1,0:T(8,128)(2,1)}, u32[]{:S(2)}, u32[]{:S(2)}) collective-permute-start(bf16[320,512]{1,0:T(8,128)(2,1)} %get-tuple-element.23), channel_id=1, source_target_pairs={{0,31},{1,0},{2,1},{3,2},{4,3},{5,4},{6,5},{7,6},{8,7},{9,8},{10,9... | collective-permute-start | bytes 983048 | tf_op jit(solution)/shard_map/ppermute | solution.py:10
  75.5 10.8 %gather_fusion = f32[3840,512]{1,0:T(8,128)} fusion(f32[640,512]{1,0:T(8,128)S(1)} %fusion.67, s32[4096]{0:T(1024)S(1)} %pad_clamp_fusion.1), kind=kCustom, calls=%fused_computation.4 | custom fusion | bytes 15744000 | tf_op jit(solution)/shard_map/jit(_take)/gather | solution.py:52
  93.3 9.7 %convolution_convert_fusion = bf16[3840,512]{1,0:T(8,128)(2,1)} fusion(bf16[512,512]{1,0:T(8,128)(2,1)S(1)} %copy-done, f32[3840,512]{1,0:T(8,128)} %gather_fusion, bf16[3840,512]{1,0:T(8,128)(2,1)} %constant_dynamic-update-slice_fusion, bf16[512,512]{1,0:T(8,128)(2,1)S(1)} %copy-done.39, f32[512]{0:T(512)S(1)} %copy-done.43, ...), kind=kOutput, calls=%fused_computation.19 | convolution fusion | flops 4044226560 | bytes 16783104 | tf_op jit(solution)/shard_map/dot_general | solution.py:54
  103.0 5.0 %fusion.63 = (f32[640]{0:T(1024)S(1)}, f32[640,512]{1,0:T(8,128)S(1)}) fusion(bf16[3840,512]{1,0:T(8,128)(2,1)} %convolution_convert_fusion, s32[3840]{0:T(1024)S(1)} %concatenate.60), kind=kOutput, calls=%fused_computation.188 | convolution fusion | flops 2519367168 | bytes 5260800 | tf_op jit(solution)/shard_map/dot_general | solution.py:60
  108.6 5.8 %scatter_custom_fusion.3 = bf16[320,512]{1,0:T(8,128)(2,1)S(1)} fusion(s32[640]{0:T(1024)S(1)} %fusion.46, bf16[640,512]{1,0:T(8,128)(2,1)S(1)} %get-tuple-element.18, bf16[]{:T(256)} %constant.182.clone.1), kind=kCustom, calls=%fused_computation.62 | custom fusion | bytes 327682 | tf_op jit(solution)/shard_map/scatter | solution.py:46
  115.1 3.1 %collective-permute-start.12 = (bf16[80,512]{1,0:T(8,128)(2,1)}, bf16[80,512]{1,0:T(8,128)(2,1)S(1)}, u32[]{:S(2)}, u32[]{:S(2)}) collective-permute-start(bf16[80,512]{1,0:T(8,128)(2,1)} %get-tuple-element.28), channel_id=1, source_target_pairs={{0,6},{1,7},{2,0},{3,1},{4,2},{5,3},{6,4},{7,5},{8,14},{9,15},{10,... | collective-permute-start | bytes 245768 | tf_op jit(solution)/shard_map/ppermute | solution.py:10
  118.3 4.8 %gather_fusion.1 = f32[960,512]{1,0:T(8,128)} fusion(f32[640,512]{1,0:T(8,128)S(1)} %fusion.68, s32[1024]{0:T(1024)S(1)} %pad_clamp_fusion.8), kind=kCustom, calls=%fused_computation.5 | custom fusion | bytes 3936000 | tf_op jit(solution)/shard_map/jit(_take)/gather | solution.py:52
  126.9 3.1 %collective-permute-done.14 = bf16[80,512]{1,0:T(8,128)(2,1)S(1)} collective-permute-done((bf16[80,512]{1,0:T(8,128)(2,1)S(1)}, bf16[80,512]{1,0:T(8,128)(2,1)S(1)}, u32[]{:S(2)}, u32[]{:S(2)}) %collective-permute-start.14) | collective-permute-done | bytes 81952 | tf_op jit(solution)/shard_map/ppermute | solution.py:10
  131.2 3.3 %convolution_convert_fusion.1 = bf16[960,512]{1,0:T(8,128)(2,1)S(1)} fusion(bf16[512,512]{1,0:T(8,128)(2,1)} %param.49, f32[960,512]{1,0:T(8,128)} %gather_fusion.1, bf16[960,512]{1,0:T(8,128)(2,1)S(1)} %constant_dynamic-update-slice_fusion.5, bf16[512,512]{1,0:T(8,128)(2,1)} %param.47, f32[512]{0:T(512)S(1)} %copy-done.44, pred[960]{0:T(1024)(128)(4,1)S(1)} %copy-done.34), kind=kOutput, calls=%fused_computation.36 | convolution fusion | flops 1011056640 | bytes 4983744 | tf_op jit(solution)/shard_map/dot_general | solution.py:54
  136.3 45.8 %all-reduce.2.cloned.1.call-done = bf16[640,512]{1,0:T(8,128)(2,1)} async-done(((bf16[640,512]{1,0:T(8,128)(2,1)}), bf16[640,512]{1,0:T(8,128)(2,1)}) %all-reduce.2.cloned.1.call-update) | async-done | bytes 655376 | tf_op jit(solution)/shard_map/psum | solution.py:150
  186.8 3.5 %collective-permute-start.17 = (bf16[640,512]{1,0:T(8,128)(2,1)S(1)}, bf16[640,512]{1,0:T(8,128)(2,1)S(1)}, u32[]{:S(2)}, u32[]{:S(2)}) collective-permute-start(bf16[640,512]{1,0:T(8,128)(2,1)S(1)} %convolution_convert_fusion.3), channel_id=1, source_target_pairs={{1,0},{2,1},{3,2},{4,3},{5,4},{6,5},{7,6},{0,7},{9,8},{10,9},{11,1... | collective-permute-start | bytes 1966088 | tf_op jit(solution)/shard_map/ppermute | solution.py:22
  192.0 11.8 %collective-permute-done.16 = bf16[640,512]{1,0:T(8,128)(2,1)S(1)} collective-permute-done((bf16[640,512]{1,0:T(8,128)(2,1)S(1)}, bf16[640,512]{1,0:T(8,128)(2,1)S(1)}, u32[]{:S(2)}, u32[]{:S(2)}) %collective-permute-start.16) | collective-permute-done | bytes 655392 | tf_op jit(solution)/shard_map/ppermute | solution.py:19
  203.9 11.7 %gather_fusion.2 = bf16[3840,512]{1,0:T(8,128)(2,1)} fusion(bf16[1920,512]{1,0:T(8,128)(2,1)S(1)} %pad_maximum_fusion, s32[4096]{0:T(1024)S(1)} %copy-done.10), kind=kCustom, calls=%fused_computation.6 | custom fusion | bytes 7879680 | tf_op jit(solution)/shard_map/jit(_take)/gather | solution.py:163
  215.6 7.8 %gather.28 = bf16[640,6,512]{2,1,0:T(8,128)(2,1)} reshape(bf16[3840,512]{1,0:T(8,128)(2,1)} %gather_fusion.2) | data formatting | bytes 7864320 | tf_op jit(solution)/shard_map/jit(_take)/gather | solution.py:163
  223.4 10.2 %multiply_reduce_fusion = (f32[640]{0:T(1024)S(1)}, f32[640,512]{0,1:T(8,128)}) fusion(f32[640,6]{0,1:T(8,128)S(1)} %copy-done.13, bf16[512,512]{1,0:T(8,128)(2,1)S(1)} %copy-done.41, bf16[640,6,512]{2,1,0:T(8,128)(2,1)} %gather.28, f32[512]{0:T(512)S(1)} %copy-done.45, f32[640,512]{1,0:T(8,128)S(1)} %copy-done.7, pred[640,6]{0,1:T(8,128)(4,1)S(1)} %copy-done.21), kind=kOutput, calls=%fused_computation.17 | convolution fusion | flops 2036530560 | bytes 7101696 | tf_op jit(solution)/shard_map/dot_general | solution.py:167
  244.9 3.0 %collective-permute-start.20 = (bf16[80,512]{1,0:T(8,128)(2,1)S(1)}, bf16[80,512]{1,0:T(8,128)(2,1)S(1)}, u32[]{:S(2)}, u32[]{:S(2)}) collective-permute-start(bf16[80,512]{1,0:T(8,128)(2,1)S(1)} %broadcast_select_fusion.1), channel_id=1, source_target_pairs={{0,7},{1,0},{2,1},{3,2},{4,3},{5,4},{6,5},{7,6},{8,15},{9,8},{10,9... | collective-permute-start | bytes 245768 | tf_op jit(solution)/shard_map/ppermute | solution.py:10
  250.0 3.5 %collective-permute-done.21 = bf16[80,512]{1,0:T(8,128)(2,1)S(1)} collective-permute-done((bf16[80,512]{1,0:T(8,128)(2,1)S(1)}, bf16[80,512]{1,0:T(8,128)(2,1)S(1)}, u32[]{:S(2)}, u32[]{:S(2)}) %collective-permute-start.21) | collective-permute-done | bytes 81952 | tf_op jit(solution)/shard_map/ppermute | solution.py:10
  253.5 2.8 %gather_fusion.4 = bf16[640,512]{1,0:T(8,128)(2,1)S(1)} fusion(bf16[960,512]{1,0:T(8,128)(2,1)S(1)} %constant_dynamic-update-slice_fusion.10, s32[1024]{0:T(1024)S(1)} %copy-done.14), kind=kCustom, calls=%fused_computation.8 | custom fusion | bytes 1313280 | tf_op jit(solution)/shard_map/jit(_take)/gather | solution.py:187
  256.3 3.3 %fusion.64 = (f32[640]{0:T(1024)S(1)}, f32[640,512]{0,1:T(8,128)}) fusion(bf16[512,512]{1,0:T(8,128)(2,1)} %param.59, f32[512]{0:T(512)S(1)} %copy-done.46, bf16[640,512]{1,0:T(8,128)(2,1)S(1)} %gather_fusion.4, pred[640]{0:T(1024)(128)(4,1)S(1)} %copy-done.33, bf16[640,512]{1,0:T(8,128)(2,1)S(1)} %copy-done.6, bf16[512,512]{1,0:T(8,128)(2,1)} %param.57), kind=kOutput, calls=%fused_computation.189 | convolution fusion | flops 674364800 | bytes 3675264 | tf_op jit(solution)/shard_map/dot_general | solution.py:193
  (241 shorter events, 63.6 us)
Async XLA Ops:
  7.2 86.1 %copy-start = (bf16[512,512]{1,0:T(8,128)(2,1)S(1)}, bf16[512,512]{1,0:T(8,128)(2,1)}, u32[]{:S(2)}) copy-start(bf16[512,512]{1,0:T(8,128)(2,1)} %param.44) | copy-start | bytes 1572868
  7.2 174.8 %all-reduce.2.cloned.1.call-start = ((), (), s32[]{:S(2)}) async-start(), calls=%async_computation | async-start | bytes 1310720 | tf_op jit(solution)/shard_map/psum | solution.py:150
  24.8 61.5 %collective-permute-start.4 = (bf16[320,512]{1,0:T(8,128)(2,1)}, bf16[320,512]{1,0:T(8,128)(2,1)}, u32[]{:S(2)}, u32[]{:S(2)}) collective-permute-start(bf16[320,512]{1,0:T(8,128)(2,1)} %get-tuple-element.24), channel_id=1, source_target_pairs={{0,30},{1,31},{2,0},{3,1},{4,2},{5,3},{6,4},{7,5},{8,6},{9,7},{10,... | collective-permute-start | bytes 983048 | tf_op jit(solution)/shard_map/ppermute | solution.py:10
  42.2 27.5 %collective-permute-start = (s32[320]{0:T(512)}, s32[320]{0:T(512)S(1)}, u32[]{:S(2)}, u32[]{:S(2)}) collective-permute-start(s32[320]{0:T(512)} %get-tuple-element.32), channel_id=1, source_target_pairs={{0,30},{1,31},{2,0},{3,1},{4,2},{5,3},{6,4},{7,5},{8,6},{9,7},{10,... | collective-permute-start | bytes 3848 | tf_op jit(solution)/shard_map/ppermute | solution.py:10
  48.7 12.1 %collective-permute-start.8 = (s32[80]{0:T(128)S(1)}, s32[80]{0:T(128)S(1)}, u32[]{:S(2)}, u32[]{:S(2)}) collective-permute-start(s32[80]{0:T(128)S(1)} %get-tuple-element.39), channel_id=1, source_target_pairs={{0,6},{1,7},{2,0},{3,1},{4,2},{5,3},{6,4},{7,5},{8,14},{9,15},{10,... | collective-permute-start | bytes 968 | tf_op jit(solution)/shard_map/ppermute | solution.py:10
  48.7 14.0 %collective-permute-start.9 = (s32[80]{0:T(128)S(1)}, s32[80]{0:T(128)S(1)}, u32[]{:S(2)}, u32[]{:S(2)}) collective-permute-start(s32[80]{0:T(128)S(1)} %get-tuple-element.38), channel_id=1, source_target_pairs={{0,7},{1,0},{2,1},{3,2},{4,3},{5,4},{6,5},{7,6},{8,15},{9,8},{10,9... | collective-permute-start | bytes 968 | tf_op jit(solution)/shard_map/ppermute | solution.py:10
  48.8 16.7 %collective-permute-start.10 = (s32[80]{0:T(128)S(1)}, s32[80]{0:T(128)S(1)}, u32[]{:S(2)}, u32[]{:S(2)}) collective-permute-start(s32[80]{0:T(128)S(1)} %get-tuple-element.37), channel_id=1, source_target_pairs={{0,1},{1,2},{2,3},{3,4},{4,5},{5,6},{6,7},{7,0},{8,9},{9,10},{10,1... | collective-permute-start | bytes 968 | tf_op jit(solution)/shard_map/ppermute | solution.py:10
  60.8 5.3 %collective-permute-start.11 = (s32[80]{0:T(128)S(1)}, s32[80]{0:T(128)S(1)}, u32[]{:S(2)}, u32[]{:S(2)}) collective-permute-start(s32[80]{0:T(128)S(1)} %get-tuple-element.36), channel_id=1, source_target_pairs={{0,2},{1,3},{2,4},{3,5},{4,6},{5,7},{6,0},{7,1},{8,10},{9,11},{10,... | collective-permute-start | bytes 968 | tf_op jit(solution)/shard_map/ppermute | solution.py:10
  62.8 12.1 %collective-permute-start.1 = (s32[320]{0:T(512)}, s32[320]{0:T(512)S(1)}, u32[]{:S(2)}, u32[]{:S(2)}) collective-permute-start(s32[320]{0:T(512)} %get-tuple-element.31), channel_id=1, source_target_pairs={{0,31},{1,0},{2,1},{3,2},{4,3},{5,4},{6,5},{7,6},{8,7},{9,8},{10,9... | collective-permute-start | bytes 3848 | tf_op jit(solution)/shard_map/ppermute | solution.py:10
  65.5 9.4 %collective-permute-start.2 = (s32[320]{0:T(512)S(1)}, s32[320]{0:T(512)S(1)}, u32[]{:S(2)}, u32[]{:S(2)}) collective-permute-start(s32[320]{0:T(512)S(1)} %get-tuple-element.30), channel_id=1, source_target_pairs={{0,1},{1,2},{2,3},{3,4},{4,5},{5,6},{6,7},{7,8},{8,9},{9,10},{10,1... | collective-permute-start | bytes 3848 | tf_op jit(solution)/shard_map/ppermute | solution.py:10
  66.1 9.1 %collective-permute-start.3 = (s32[320]{0:T(512)S(1)}, s32[320]{0:T(512)S(1)}, u32[]{:S(2)}, u32[]{:S(2)}) collective-permute-start(s32[320]{0:T(512)S(1)} %get-tuple-element.29), channel_id=1, source_target_pairs={{0,2},{1,3},{2,4},{3,5},{4,6},{5,7},{6,8},{7,9},{8,10},{9,11},{10,... | collective-permute-start | bytes 3848 | tf_op jit(solution)/shard_map/ppermute | solution.py:10
  69.7 18.4 %collective-permute-start.5 = (bf16[320,512]{1,0:T(8,128)(2,1)}, bf16[320,512]{1,0:T(8,128)(2,1)}, u32[]{:S(2)}, u32[]{:S(2)}) collective-permute-start(bf16[320,512]{1,0:T(8,128)(2,1)} %get-tuple-element.23), channel_id=1, source_target_pairs={{0,31},{1,0},{2,1},{3,2},{4,3},{5,4},{6,5},{7,6},{8,7},{9,8},{10,9... | collective-permute-start | bytes 983048 | tf_op jit(solution)/shard_map/ppermute | solution.py:10
  74.9 14.9 %collective-permute-start.6 = (bf16[320,512]{1,0:T(8,128)(2,1)}, bf16[320,512]{1,0:T(8,128)(2,1)}, u32[]{:S(2)}, u32[]{:S(2)}) collective-permute-start(bf16[320,512]{1,0:T(8,128)(2,1)} %get-tuple-element.22), channel_id=1, source_target_pairs={{0,1},{1,2},{2,3},{3,4},{4,5},{5,6},{6,7},{7,8},{8,9},{9,10},{10,1... | collective-permute-start | bytes 983048 | tf_op jit(solution)/shard_map/ppermute | solution.py:10
  74.9 16.7 %collective-permute-start.7 = (bf16[320,512]{1,0:T(8,128)(2,1)S(1)}, bf16[320,512]{1,0:T(8,128)(2,1)}, u32[]{:S(2)}, u32[]{:S(2)}) collective-permute-start(bf16[320,512]{1,0:T(8,128)(2,1)S(1)} %get-tuple-element.21), channel_id=1, source_target_pairs={{0,2},{1,3},{2,4},{3,5},{4,6},{5,7},{6,8},{7,9},{8,10},{9,11},{10,... | collective-permute-start | bytes 983048 | tf_op jit(solution)/shard_map/ppermute | solution.py:10
  115.1 9.3 %collective-permute-start.12 = (bf16[80,512]{1,0:T(8,128)(2,1)}, bf16[80,512]{1,0:T(8,128)(2,1)S(1)}, u32[]{:S(2)}, u32[]{:S(2)}) collective-permute-start(bf16[80,512]{1,0:T(8,128)(2,1)} %get-tuple-element.28), channel_id=1, source_target_pairs={{0,6},{1,7},{2,0},{3,1},{4,2},{5,3},{6,4},{7,5},{8,14},{9,15},{10,... | collective-permute-start | bytes 245768 | tf_op jit(solution)/shard_map/ppermute | solution.py:10
  123.1 3.8 %collective-permute-start.13 = (bf16[80,512]{1,0:T(8,128)(2,1)S(1)}, bf16[80,512]{1,0:T(8,128)(2,1)S(1)}, u32[]{:S(2)}, u32[]{:S(2)}) collective-permute-start(bf16[80,512]{1,0:T(8,128)(2,1)S(1)} %get-tuple-element.27), channel_id=1, source_target_pairs={{0,7},{1,0},{2,1},{3,2},{4,3},{5,4},{6,5},{7,6},{8,15},{9,8},{10,9... | collective-permute-start | bytes 245768 | tf_op jit(solution)/shard_map/ppermute | solution.py:10
  124.1 6.0 %collective-permute-start.14 = (bf16[80,512]{1,0:T(8,128)(2,1)S(1)}, bf16[80,512]{1,0:T(8,128)(2,1)S(1)}, u32[]{:S(2)}, u32[]{:S(2)}) collective-permute-start(bf16[80,512]{1,0:T(8,128)(2,1)S(1)} %get-tuple-element.26), channel_id=1, source_target_pairs={{0,1},{1,2},{2,3},{3,4},{4,5},{5,6},{6,7},{7,0},{8,9},{9,10},{10,1... | collective-permute-start | bytes 245768 | tf_op jit(solution)/shard_map/ppermute | solution.py:10
  124.1 7.1 %collective-permute-start.15 = (bf16[80,512]{1,0:T(8,128)(2,1)S(1)}, bf16[80,512]{1,0:T(8,128)(2,1)S(1)}, u32[]{:S(2)}, u32[]{:S(2)}) collective-permute-start(bf16[80,512]{1,0:T(8,128)(2,1)S(1)} %get-tuple-element.25), channel_id=1, source_target_pairs={{0,2},{1,3},{2,4},{3,5},{4,6},{5,7},{6,0},{7,1},{8,10},{9,11},{10,... | collective-permute-start | bytes 245768 | tf_op jit(solution)/shard_map/ppermute | solution.py:10
  186.8 17.0 %collective-permute-start.16 = (bf16[640,512]{1,0:T(8,128)(2,1)S(1)}, bf16[640,512]{1,0:T(8,128)(2,1)S(1)}, u32[]{:S(2)}, u32[]{:S(2)}) collective-permute-start(bf16[640,512]{1,0:T(8,128)(2,1)S(1)} %convolution_convert_fusion.3), channel_id=1, source_target_pairs={{0,1},{1,2},{2,3},{3,4},{4,5},{5,6},{6,7},{7,0},{8,9},{9,10},{10,1... | collective-permute-start | bytes 1966088 | tf_op jit(solution)/shard_map/ppermute | solution.py:19
  186.8 16.9 %collective-permute-start.17 = (bf16[640,512]{1,0:T(8,128)(2,1)S(1)}, bf16[640,512]{1,0:T(8,128)(2,1)S(1)}, u32[]{:S(2)}, u32[]{:S(2)}) collective-permute-start(bf16[640,512]{1,0:T(8,128)(2,1)S(1)} %convolution_convert_fusion.3), channel_id=1, source_target_pairs={{1,0},{2,1},{3,2},{4,3},{5,4},{6,5},{7,6},{0,7},{9,8},{10,9},{11,1... | collective-permute-start | bytes 1966088 | tf_op jit(solution)/shard_map/ppermute | solution.py:22
  241.1 8.7 %collective-permute-start.18 = (bf16[80,512]{1,0:T(8,128)(2,1)S(1)}, bf16[80,512]{1,0:T(8,128)(2,1)S(1)}, u32[]{:S(2)}, u32[]{:S(2)}) collective-permute-start(bf16[80,512]{1,0:T(8,128)(2,1)S(1)} %broadcast_select_fusion.3), channel_id=1, source_target_pairs={{0,2},{1,3},{2,4},{3,5},{4,6},{5,7},{6,0},{7,1},{8,10},{9,11},{10,... | collective-permute-start | bytes 245768 | tf_op jit(solution)/shard_map/ppermute | solution.py:10
  243.4 6.5 %collective-permute-start.19 = (bf16[80,512]{1,0:T(8,128)(2,1)S(1)}, bf16[80,512]{1,0:T(8,128)(2,1)S(1)}, u32[]{:S(2)}, u32[]{:S(2)}) collective-permute-start(bf16[80,512]{1,0:T(8,128)(2,1)S(1)} %broadcast_select_fusion.2), channel_id=1, source_target_pairs={{0,1},{1,2},{2,3},{3,4},{4,5},{5,6},{6,7},{7,0},{8,9},{9,10},{10,1... | collective-permute-start | bytes 245768 | tf_op jit(solution)/shard_map/ppermute | solution.py:10
  244.9 5.1 %collective-permute-start.20 = (bf16[80,512]{1,0:T(8,128)(2,1)S(1)}, bf16[80,512]{1,0:T(8,128)(2,1)S(1)}, u32[]{:S(2)}, u32[]{:S(2)}) collective-permute-start(bf16[80,512]{1,0:T(8,128)(2,1)S(1)} %broadcast_select_fusion.1), channel_id=1, source_target_pairs={{0,7},{1,0},{2,1},{3,2},{4,3},{5,4},{6,5},{7,6},{8,15},{9,8},{10,9... | collective-permute-start | bytes 245768 | tf_op jit(solution)/shard_map/ppermute | solution.py:10
  248.7 4.8 %collective-permute-start.21 = (bf16[80,512]{1,0:T(8,128)(2,1)S(1)}, bf16[80,512]{1,0:T(8,128)(2,1)S(1)}, u32[]{:S(2)}, u32[]{:S(2)}) collective-permute-start(bf16[80,512]{1,0:T(8,128)(2,1)S(1)} %broadcast_select_fusion), channel_id=1, source_target_pairs={{0,6},{1,7},{2,0},{3,1},{4,2},{5,3},{6,4},{7,5},{8,14},{9,15},{10,... | collective-permute-start | bytes 245768 | tf_op jit(solution)/shard_map/ppermute | solution.py:10
  (46 other events, 502.8 us)
Sparse Core Ops, SparseCore 0:
  136.3 45.6 all-reduce.1
where the time goes:
time: 270 us
  local copies, waits for them, and re-layouts  94.4 us (35%)
  waiting for transfers between devices  68.5 us (25%)
  matrix products  39 us (14%)
  starting transfers between devices  32.3 us (12%)
  other arithmetic  20.4 us (8%)
  between operations  15.1 us (6%)
    psum x1, waiting for transfers between devices, on_device(): lax.psum(partial_sum.astype(jnp.bfloat16), 'grp').astype(jnp.float32)  45.8 us
    ppermute x20, starting transfers between devices, from_behind(): return lax.ppermute(value, axis, pairs)  28.7 us
    gather x2, local copies, waits for them, and re-layouts, on_device(): jnp.take(rim, local.reshape(-1), axis=0)  19.5 us
    scatter x2, local copies, waits for them, and re-layouts, fill_slots(): jnp.zeros((total, rows.shape[1]), rows.dtype).at[position]  18.2 us
    gather x2, local copies, waits for them, and re-layouts, receive_messages(): picked = jnp.take(parent_terms, jnp.maximum(labels, 0), axis=0)  15.6 us
    scatter x2, local copies, waits for them, and re-layouts, fill_slots(): jnp.full((total,), -1, jnp.int32).at[position].set(parents, mode='drop')  14 us
    dot_general x2, matrix products, receive_messages(): jnp.dot(hidden.astype(jnp.bfloat16), w_out, preferred_element_type=jnp.fl...  13 us
    ppermute x1, waiting for transfers between devices, extended(): lax.ppermute(lax.slice_in_dim(block, block.shape[dim] - width, None, axis...  11.8 us
  transfers between devices with their start and end apart: 23, of which 8 were waited for; matrix products, arithmetic and copies ran while one was open for 21% of the time, Pallas kernels for 0%

commit v1 on v0

v1 whole, which is shorter than its diff:
```python
import functools

import jax
import jax.numpy as jnp
from jax import lax
from jax.experimental import pallas as pl
from jax.experimental.pallas import tpu as pltpu
from jax.sharding import PartitionSpec as P

MESH = pl.DeviceIdType.MESH
OFFSETS = (-2, -1, 1, 2)
LANES = 128
BF = jnp.bfloat16
F32 = jnp.float32
I32 = jnp.int32


def dot(a, b):
    return jnp.dot(a, b, preferred_element_type=F32)


def round_up(value, step):
    return -(-value // step) * step


def silu(x):
    half = 0.5 * x
    return half + half * jnp.tanh(half)


def layer_norm(values, gain):
    center = values - jnp.mean(values, axis=-1, keepdims=True)
    spread = jnp.mean(center * center, axis=-1, keepdims=True)
    return center * lax.rsqrt(spread + 1e-05) * gain


def iota(shape, dim):
    return lax.broadcasted_iota(I32, shape, dim)


def where_equal(a, b):
    return (a == b).astype(F32).astype(BF)


def pick_matrix(labels, total):
    return where_equal(labels, iota((labels.shape[0], total), 1))


def member_matrix(labels, total):
    return where_equal(labels, iota((total, labels.shape[1]), 0))


def places(codes):
    rows = codes.shape[0]
    size = round_up(4 * rows, LANES)
    parts = [(codes == float(c + 1)).astype(F32) for c in range(4)]
    if size > 4 * rows:
        parts.append(jnp.zeros((size - 4 * rows, LANES), F32))
    chosen = jnp.concatenate(parts, axis=0).astype(BF)
    before = (iota((LANES, LANES), 0) < iota((LANES, LANES), 1)).astype(F32).astype(BF)
    within = dot(chosen, before)
    totals = dot(chosen, jnp.ones((LANES, LANES), BF)).astype(BF)
    row, col = iota((size, size), 0), iota((size, size), 1)
    lowest = jnp.zeros((size, size), I32)
    for c in range(1, 5):
        lowest = jnp.where(row >= c * rows, c * rows, lowest)
    earlier = ((col >= lowest) & (col < row)).astype(F32).astype(BF)
    placed = within + dot(earlier, totals)
    result = jnp.zeros((rows, LANES), F32)
    for c in range(4):
        result = jnp.where(codes == float(c + 1), placed[c * rows : (c + 1) * rows], result)
    return result


def as_row(table, blocks):
    return jnp.concatenate([table[b : b + 1, :] for b in range(blocks)], axis=1)


def as_column(turned, first, blocks):
    return jnp.concatenate([turned[:, first + b : first + b + 1] for b in range(blocks)], axis=0)


def turn(parts):
    rows = sum(part.shape[0] for part in parts)
    fill = round_up(rows, LANES) - rows
    if fill:
        parts = parts + [jnp.zeros((fill, LANES), F32)]
    return jnp.concatenate(parts, axis=0).T


def slot_labels(code_row, place_row, parent_row, place_column):
    key = jnp.where(code_row > 0, (code_row - 1) * 8 + (place_row >> 7), -1)
    hit = key == iota((32, key.shape[1]), 0)
    value = parent_row + 1
    high = jnp.where(hit, (value >> 5).astype(F32), 0.0).astype(BF)
    low = jnp.where(hit, (value & 31).astype(F32), 0.0).astype(BF)
    spread = where_equal(place_column & (LANES - 1), iota((place_column.shape[0], LANES), 1))
    return 32.0 * dot(high, spread) + dot(low, spread) - 1.0


def kernel(
    sizes,
    meta,
    fine,
    mid,
    coarse,
    neighbours,
    mask,
    up_child_w,
    up_parent_w,
    up_out_w,
    up_bias,
    up_gain,
    mid_child_w,
    mid_parent_w,
    mid_out_w,
    mid_bias,
    mid_gain,
    same_self_w,
    same_other_w,
    same_out_w,
    same_bias,
    same_gain,
    down_child_w,
    down_parent_w,
    down_out_w,
    down_bias,
    down_gain,
    mid_out,
    coarse_out,
    fine_send,
    fine_got,
    fine_label_send,
    fine_label_got,
    mid_send,
    mid_got,
    mid_label_send,
    mid_label_got,
    sum_send,
    sum_got,
    rim,
    coarse_all,
    back_send,
    back_got,
    fine_row,
    fine_column,
    got_row,
    got_column,
    mid_terms,
    coarse_terms,
    fine_total,
    mid_total,
    mid_new,
    send_sem,
    recv_sem,
):
    groups, members, tile = sizes
    everyone = groups * members
    fine_count, width = fine.shape
    mid_count = mid.shape[0]
    coarse_count = coarse.shape[0]
    fine_cap, mid_cap = fine_count // 8, mid_count // 8
    fine_step, mid_step = round_up(fine_cap, LANES), round_up(mid_cap, LANES)
    fine_blocks, mid_blocks = fine_count // LANES, mid_count // LANES
    fine_rows, mid_rows = round_up(fine_blocks, 8), round_up(mid_blocks, 8)
    chunk = coarse_count // groups
    slots = neighbours.shape[1]
    g, d = lax.axis_index("grp"), lax.axis_index("dev")
    here = g * members + d
    ring = d * groups + g

    def along_all(offset):
        to = lax.rem(here + offset + everyone, everyone)
        return (lax.div(to, members), lax.rem(to, members))

    def along_dev(offset):
        return (g, lax.rem(d + offset + members, members))

    def along_grp(offset):
        return (lax.rem(g + offset + groups, groups), d)

    def along_ring(offset):
        to = lax.rem(ring + offset + everyone, everyone)
        return (lax.rem(to, groups), lax.div(to, groups))

    hops = [j for j in range(-groups, groups + 1) if j]
    greeted = [along_all(o) for o in OFFSETS]
    greeted += [along_dev(o) for o in OFFSETS]
    greeted += [along_ring(j) for j in hops]
    barrier = pltpu.get_barrier_semaphore()
    for device in greeted:
        pl.semaphore_signal(barrier, inc=1, device_id=device, device_id_type=MESH)

    def remote(index, source, target, device):
        return pltpu.make_async_remote_copy(
            src_ref=source,
            dst_ref=target,
            send_sem=send_sem.at[index],
            recv_sem=recv_sem.at[index],
            device_id=device,
            device_id_type=MESH,
        )

    started = []

    def start(copy):
        copy.start()
        started.append(copy)
        return copy

    fine_codes = meta[0:fine_rows, :]
    fine_parents = meta[fine_rows : 2 * fine_rows, :]
    mid_codes = meta[2 * fine_rows : 2 * fine_rows + mid_rows, :]
    mid_parents = meta[2 * fine_rows + mid_rows : 2 * fine_rows + 2 * mid_rows, :]
    fine_places = places(fine_codes)
    mid_places = places(mid_codes)
    fine_own = jnp.where(fine_codes == 0.0, fine_parents, -1.0)
    mid_own = jnp.where(mid_codes == 0.0, mid_parents, -1.0)
    mid_choice = jnp.where(mid_codes > 0.0, (mid_codes - 1.0) * mid_cap + mid_places, -1.0)
    turned = turn([fine_places, fine_own, mid_places, mid_own, mid_choice]).astype(I32)
    at = 0
    fine_place_column = as_column(turned, at, fine_blocks)
    at += fine_rows
    for b in range(fine_blocks):
        fine_column[b * LANES : (b + 1) * LANES, :] = turned[:, at + b : at + b + 1]
    at += fine_rows
    mid_place_column = as_column(turned, at, mid_blocks)
    at += mid_rows
    mid_own_column = as_column(turned, at, mid_blocks)
    at += mid_rows
    mid_choice_column = as_column(turned, at, mid_blocks)
    fine_code_row = as_row(fine_codes, fine_blocks).astype(I32)
    fine_place_row = as_row(fine_places, fine_blocks).astype(I32)
    fine_own_row = as_row(fine_own, fine_blocks).astype(I32)
    for t in range(fine_count // tile):
        fine_row[t : t + 1, :] = fine_own_row[:, t * tile : (t + 1) * tile]
    mid_code_row = as_row(mid_codes, mid_blocks).astype(I32)
    mid_place_row = as_row(mid_places, mid_blocks).astype(I32)
    mid_own_row = as_row(mid_own, mid_blocks).astype(I32)
    fine_label_send[...] = slot_labels(
        fine_code_row,
        fine_place_row,
        as_row(fine_parents, fine_blocks).astype(I32),
        fine_place_column,
    )
    mid_label_send[...] = slot_labels(
        mid_code_row,
        mid_place_row,
        as_row(mid_parents, mid_blocks).astype(I32),
        mid_place_column,
    )
    for c in range(4):
        if fine_step > fine_cap:
            low, high = c * fine_step + fine_cap, (c + 1) * fine_step
            fine_got[low:high, :] = jnp.zeros((high - low, width), BF)
        if mid_step > mid_cap:
            low, high = c * mid_step + mid_cap, (c + 1) * mid_step
            mid_got[low:high, :] = jnp.zeros((high - low, width), BF)
    filled = (2 * groups + 1) * chunk
    if rim.shape[0] > filled:
        rim[filled:, :] = jnp.zeros((rim.shape[0] - filled, rim.shape[1]), BF)

    pl.semaphore_wait(barrier, len(greeted))

    fine_copies, fine_label_copies, mid_label_copies = [None] * 4, [], []
    for c, offset in enumerate(OFFSETS):
        rows = slice(8 * c, 8 * c + 8)
        fine_label_copies.append(
            start(remote(c, fine_label_send.at[rows], fine_label_got.at[rows], along_all(offset)))
        )
        mid_label_copies.append(
            start(remote(4 + c, mid_label_send.at[rows], mid_label_got.at[rows], along_dev(offset)))
        )
    for c in (0, 3, 1, 2):
        wanted = jnp.where(fine_code_row == c + 1, fine_place_row, -1)
        packed = dot(member_matrix(wanted, fine_cap), fine[...])
        fine_send[c * fine_cap : (c + 1) * fine_cap, :] = packed.astype(BF)
        fine_copies[c] = start(
            remote(
                8 + c,
                fine_send.at[c * fine_cap : (c + 1) * fine_cap],
                fine_got.at[c * fine_step : c * fine_step + fine_cap],
                along_all(OFFSETS[c]),
            )
        )
    mid_terms[...] = dot(mid[...], up_parent_w[...]).astype(BF)
    coarse_terms[...] = dot(coarse[...], mid_parent_w[...]).astype(BF)

    def fine_part(rows, column, row):
        hidden = silu(
            dot(rows, up_child_w[...]) + dot(pick_matrix(column, mid_count), mid_terms[...]) + up_bias[...]
        ).astype(BF)
        return dot(member_matrix(row, mid_count), hidden)

    fine_total[...] = jnp.zeros_like(fine_total)

    def own_tile(t, carry):
        first = pl.multiple_of(t * tile, tile)
        fine_total[...] += fine_part(
            fine[pl.ds(first, tile), :], fine_column[pl.ds(first, tile), :], fine_row[pl.ds(t, 1), :]
        )
        return carry

    lax.fori_loop(0, fine_count // tile, own_tile, 0)

    for copy in fine_label_copies + mid_label_copies:
        copy.wait_recv()
    fine_got_labels = fine_label_got[...]
    mid_got_labels = mid_label_got[...]
    got_turned = turn([fine_got_labels, mid_got_labels]).astype(I32)
    per = fine_step // LANES
    for c in range(4):
        for s in range(per):
            low = c * fine_step + s * LANES
            got_column[low : low + LANES, :] = got_turned[:, 8 * c + s : 8 * c + s + 1]
            got_row[c : c + 1, s * LANES : (s + 1) * LANES] = fine_got_labels[
                8 * c + s : 8 * c + s + 1, :
            ].astype(I32)
    mid_per = mid_step // LANES
    mid_got_column = jnp.concatenate(
        [as_column(got_turned, 32 + 8 * c, mid_per) for c in range(4)], axis=0
    )
    mid_got_row = jnp.concatenate(
        [mid_got_labels[8 * c + s : 8 * c + s + 1, :] for c in range(4) for s in range(mid_per)], axis=1
    ).astype(I32)
    for c in (1, 2, 0, 3):
        fine_copies[c].wait_recv()
        low = c * fine_step
        fine_total[...] += fine_part(
            fine_got[low : low + fine_step, :],
            got_column[low : low + fine_step, :],
            got_row[c : c + 1, :],
        )
    fine_sum = dot(fine_total[...].astype(BF), up_out_w[...])
    mid_new[...] = (mid[...].astype(F32) + layer_norm(fine_sum, up_gain[...])).astype(BF)

    mid_copies = []
    for c, offset in enumerate(OFFSETS):
        wanted = jnp.where(mid_code_row == c + 1, mid_place_row, -1)
        packed = dot(member_matrix(wanted, mid_cap), mid_new[...])
        mid_send[c * mid_cap : (c + 1) * mid_cap, :] = packed.astype(BF)
        mid_copies.append(
            start(
                remote(
                    12 + c,
                    mid_send.at[c * mid_cap : (c + 1) * mid_cap],
                    mid_got.at[c * mid_step : c * mid_step + mid_cap],
                    along_dev(offset),
                )
            )
        )

    def mid_part(rows, column, row):
        hidden = silu(
            dot(rows, mid_child_w[...])
            + dot(pick_matrix(column, coarse_count), coarse_terms[...])
            + mid_bias[...]
        ).astype(BF)
        return dot(member_matrix(row, coarse_count), hidden)

    mid_total[...] = mid_part(mid_new[...], mid_own_column, mid_own_row)
    for copy in mid_copies:
        copy.wait_recv()
    mid_total[...] += mid_part(mid_got[...], mid_got_column, mid_got_row)

    sum_send[...] = mid_total[...].astype(BF)
    sum_copies = []
    for k in range(1, groups):
        to = along_grp(k)
        sum_copies.append(
            start(
                remote(
                    16 + k - 1,
                    sum_send.at[pl.ds(pl.multiple_of(to[0] * chunk, chunk), chunk)],
                    sum_got.at[(k - 1) * chunk : k * chunk],
                    to,
                )
            )
        )
    mine = pl.ds(pl.multiple_of(g * chunk, chunk), chunk)
    child_terms = dot(mid_new[...], down_child_w[...]) + down_bias[...]
    hidden_sum = mid_total[mine, :]
    for k in range(1, groups):
        sum_copies[k - 1].wait_recv()
        hidden_sum += sum_got[(k - 1) * chunk : k * chunk, :].astype(F32)
    coarse_sum = dot(hidden_sum.astype(BF), mid_out_w[...])
    coarse_new = (coarse[mine, :].astype(F32) + layer_norm(coarse_sum, mid_gain[...])).astype(BF)

    first = 16 + groups - 1
    own_rim = rim.at[groups * chunk : (groups + 1) * chunk]
    own_rim[...] = dot(coarse_new, same_other_w[...]).astype(BF)
    rim_copies = []
    for n, j in enumerate(hops):
        rim_copies.append(
            start(
                remote(
                    first + n,
                    own_rim,
                    rim.at[(groups - j) * chunk : (groups - j + 1) * chunk],
                    along_ring(j),
                )
            )
        )
    self_terms = dot(coarse_new, same_self_w[...]) + same_bias[...]
    total_rows = members * coarse_count
    local = neighbours[mine, :] - (ring * chunk - groups * chunk)
    local = jnp.where(local < 0, local + total_rows, local)
    local = jnp.where(local >= total_rows, local - total_rows, local)
    used = mask[mine, :].astype(F32)
    for copy in rim_copies:
        copy.wait_recv()
    same_hidden = jnp.zeros((chunk, width), F32)
    for k in range(slots):
        picked = dot(pick_matrix(local[:, k : k + 1], rim.shape[0]), rim[...])
        same_hidden += silu(self_terms + picked) * used[:, k : k + 1]
    same_sum = dot(same_hidden.astype(BF), same_out_w[...])
    coarse_all[mine, :] = (
        coarse_new.astype(F32) + layer_norm(same_sum, same_gain[...])
    ).astype(BF)

    first += len(hops)
    for k in range(1, groups):
        start(remote(first + k - 1, coarse_all.at[mine], coarse_all.at[mine], along_grp(k)))
    for k in range(1, groups):
        source = along_grp(-k)[0]
        theirs = pl.ds(pl.multiple_of(source * chunk, chunk), chunk)
        remote(first + k - 1, coarse_all.at[theirs], coarse_all.at[theirs], along_grp(-k)).wait_recv()
    coarse_out[...] = coarse_all[...]
    down_terms = dot(coarse_all[...], down_parent_w[...]).astype(BF)
    back_send[...] = dot(pick_matrix(mid_got_column, coarse_count), down_terms).astype(BF)
    first += groups - 1
    back_copies = []
    for c, offset in enumerate(OFFSETS):
        back_copies.append(
            start(
                remote(
                    first + c,
                    back_send.at[c * mid_step : c * mid_step + mid_cap],
                    back_got.at[c * mid_cap : (c + 1) * mid_cap],
                    along_dev(-offset),
                )
            )
        )
    child_terms += dot(pick_matrix(mid_own_column, coarse_count), down_terms)
    for copy in back_copies:
        copy.wait_recv()
    child_terms += dot(pick_matrix(mid_choice_column, 4 * mid_cap), back_got[...])
    down_messages = dot(silu(child_terms).astype(BF), down_out_w[...])
    mid_out[...] = (
        mid_new[...].astype(F32) + layer_norm(down_messages, down_gain[...])
    ).astype(BF)
    for copy in started:
        copy.wait_send()


def direction(owner, index, total):
    relative = (owner - index) % total
    code = jnp.where(relative == 0, 0, 5)
    for c, offset in enumerate(OFFSETS):
        code = jnp.where(relative == offset % total, c + 1, code)
    return code


def table(values, fill):
    values = values.reshape(-1, LANES)
    rows = round_up(values.shape[0], 8)
    return jnp.pad(values, ((0, rows - values.shape[0]), (0, 0)), constant_values=fill)


def on_device(
    fine_nodes,
    mid_nodes,
    coarse_nodes,
    fine_owner,
    fine_parent,
    mid_owner,
    mid_parent,
    neighbours,
    neighbour_mask,
    *weights,
):
    groups = lax.axis_size("grp")
    members = lax.axis_size("dev")
    dev_index = lax.axis_index("dev")
    here = lax.axis_index("grp") * members + dev_index
    meta = jnp.concatenate(
        [
            table(direction(fine_owner[:, 0], here, groups * members), 5),
            table(fine_parent, 0),
            table(direction(mid_owner[:, 0], dev_index, members), 5),
            table(mid_parent, 0),
        ],
        axis=0,
    ).astype(F32)
    weights = [w if w.ndim == 2 else w[None, :] for w in weights]
    fine_count, width = fine_nodes.shape
    mid_count, coarse_count = mid_nodes.shape[0], coarse_nodes.shape[0]
    fine_cap, mid_cap = fine_count // 8, mid_count // 8
    fine_step, mid_step = round_up(fine_cap, LANES), round_up(mid_cap, LANES)
    chunk = coarse_count // groups
    rim_rows = round_up((2 * groups + 1) * chunk, LANES)
    tile = 512 if fine_count % 512 == 0 else LANES
    copies = 16 + (groups - 1) + 2 * groups + (groups - 1) + 4
    vmem = pl.BlockSpec(memory_space=pltpu.VMEM)
    operands = (meta, fine_nodes, mid_nodes, coarse_nodes, neighbours, neighbour_mask, *weights)
    return pl.pallas_call(
        functools.partial(kernel, (groups, members, tile)),
        out_shape=(
            jax.ShapeDtypeStruct((mid_count, width), BF),
            jax.ShapeDtypeStruct((coarse_count, width), BF),
        ),
        in_specs=[vmem] * len(operands),
        out_specs=(vmem, vmem),
        scratch_shapes=[
            pltpu.VMEM((4 * fine_cap, width), BF),
            pltpu.VMEM((4 * fine_step, width), BF),
            pltpu.VMEM((32, LANES), F32),
            pltpu.VMEM((32, LANES), F32),
            pltpu.VMEM((4 * mid_cap, width), BF),
            pltpu.VMEM((4 * mid_step, width), BF),
            pltpu.VMEM((32, LANES), F32),
            pltpu.VMEM((32, LANES), F32),
            pltpu.VMEM((coarse_count, width), BF),
            pltpu.VMEM(((groups - 1) * chunk, width), BF),
            pltpu.VMEM((rim_rows, width), BF),
            pltpu.VMEM((coarse_count, width), BF),
            pltpu.VMEM((4 * mid_step, width), BF),
            pltpu.VMEM((4 * mid_cap, width), BF),
            pltpu.VMEM((fine_count // tile, tile), I32),
            pltpu.VMEM((fine_count, 1), I32),
            pltpu.VMEM((4, fine_step), I32),
            pltpu.VMEM((4 * fine_step, 1), I32),
            pltpu.VMEM((mid_count, width), BF),
            pltpu.VMEM((coarse_count, width), BF),
            pltpu.VMEM((mid_count, width), F32),
            pltpu.VMEM((coarse_count, width), F32),
            pltpu.VMEM((mid_count, width), BF),
            pltpu.SemaphoreType.DMA((copies,)),
            pltpu.SemaphoreType.DMA((copies,)),
        ],
        compiler_params=pltpu.CompilerParams(
            collective_id=0, has_side_effects=True, vmem_limit_bytes=56 * 1024 * 1024
        ),
    )(*operands)


def solution(mesh):
    nodes, split = P(("grp", "dev"), None), P(("grp", "dev"))
    part = P("dev", None)
    in_specs = (nodes, nodes, part, nodes, split, nodes, split, part, part) + (P(),) * 20
    return jax.shard_map(
        on_device, mesh=mesh, in_specs=in_specs, out_specs=(nodes, part), check_vma=False
    )
```

time: 270 us -> 104 us (0.39)
  Pallas kernels: 0 us -> 92.8 us
  local copies, waits for them, and re-layouts: 94.4 us -> 7.18 us
  waiting for transfers between devices: 68.5 us -> 0 us
  matrix products: 39 us -> 0 us
  starting transfers between devices: 32.3 us -> 0 us
  other arithmetic: 20.4 us -> 2.79 us
  between operations: 15.1 us -> 0.66 us
    pallas_call x0 -> x1, Pallas kernels: none -> 92.8 us  [on_device(): pl.pallas_call(functools.partial(kernel, (groups, members, tile)), out_sh...]
    psum x1 -> x0, waiting for transfers between devices: 45.8 us -> none  [on_device(): lax.psum(partial_sum.astype(jnp.bfloat16), 'grp').astype(jnp.float32)]
    gather x10 -> x0, local copies, waits for them, and re-layouts: 43.6 us -> none  [the longest x2 19.5 us: on_device(): jnp.take(rim, local.reshape(-1), axis=0)]
    dot_general x11 -> x0, matrix products: 39 us -> none  [the longest x2 13 us: receive_messages(): jnp.dot(hidden.astype(jnp.bfloat16), w_out, preferred_element_type=jnp.fl...]
    ppermute x22 -> x0, starting transfers between devices: 32.3 us -> none  [the longest x20 28.7 us: from_behind(): return lax.ppermute(value, axis, pairs)]
    scatter x4 -> x0, local copies, waits for them, and re-layouts: 32.2 us -> none  [the longest x2 18.2 us: fill_slots(): jnp.zeros((total, rows.shape[1]), rows.dtype).at[position]]
    ppermute x22 -> x0, waiting for transfers between devices: 22.7 us -> none  [the longest x1 11.8 us: extended(): lax.ppermute(lax.slice_in_dim(block, block.shape[dim] - width, None, axis...]
    reduce_sum x7 -> x0, other arithmetic: 4.44 us -> none  [the longest x4 2.26 us: layer_norm(): spread = jnp.mean(center * center, axis=-1, keepdims=True)]
  transfers between devices with their start and end apart: 23 -> 0, of which waited for: 8 -> 0; matrix products, arithmetic and copies ran while one was open for 21% -> 0% of each run, Pallas kernels for 0% -> 0%
where the time goes in v1:
time: 104 us; the launch traced here: 103 us
  Pallas kernels  92.8 us (89%)
  local copies, waits for them, and re-layouts  7.18 us (7%)
  other arithmetic  2.79 us (3%)
    pallas_call x1, Pallas kernels, on_device(): pl.pallas_call(functools.partial(kernel, (groups, members, tile)), out_sh...  92.8 us
    unnamed x4, local copies, waits for them, and re-layouts  7.18 us

profile of v1, /device:TPU:0, one launch (start us, length us, event | category | flops | bytes accessed | tf_op | source)
XLA Modules:
  0.0 103.4 jit_solution(14428978180200578189)
XLA Ops:
  0.6 0.7 subtract_reduce_fusion.1
  1.4 0.7 subtract_reduce_fusion
  2.1 1.3 %fusion.meta = f32[64,128]{1,0:T(8,128)} fusion(s32[5,128]{1,0:T(8,128)} %bitcast.19, s32[5,128]{1,0:T(8,128)S(1)} %select_select_fusion.1, s32[20,128]{1,0:T(8,128)} %bitcast.18, s32[20,128]{1,0:T(8,128)S(1)} %select_select_fusion), kind=kLoop, calls=%fused_computation.3 | loop fusion | flops 81920 | bytes 58368 | tf_op jit(solution)/shard_map/convert_element_type | solution.py:494
  3.4 1.6 %copy.31.neighbours = s32[640,6]{1,0:T(8,128)} copy(s32[640,6]{0,1:T(8,128)} %param.36) | data formatting | bytes 30720 | tf_op args[7]
  5.1 1.6 %copy.32.mask = s32[640,6]{1,0:T(8,128)} copy(s32[640,6]{0,1:T(8,128)} %param.37) | data formatting | bytes 30720 | tf_op args[8]
  6.7 92.8 %shard_map.284 = (bf16[640,512]{1,0:T(8,128)(2,1)}, bf16[640,512]{1,0:T(8,128)(2,1)}) custom-call(f32[64,128]{1,0:T(8,128)} %fusion.meta, bf16[2560,512]{1,0:T(8,128)(2,1)} %fine.1, bf16[640,512]{1,0:T(8,128)(2,1)} %mid.1, bf16[640,512]{1,0:T(8,128)(2,1)} %coarse.1, s32[640,6]{1,0:T(8,128)} %copy.31.neighbours, s32[640,6]{1,0:T(8,128)} %copy.32.mask, ...), custom_call_target="tpu_custom_call" | custom-call | tf_op jit(solution)/shard_map/pallas_call | solution.py:506
  99.5 2.0 %copy.35 = bf16[640,512]{1,0:T(8,128)(2,1)} copy(bf16[640,512]{1,0:T(8,128)(2,1)} %get-tuple-element.4) | data formatting | bytes 1310720
  101.5 2.0 %copy.36 = bf16[640,512]{1,0:T(8,128)(2,1)} copy(bf16[640,512]{1,0:T(8,128)(2,1)} %get-tuple-element.5) | data formatting | bytes 1310720
  (2 shorter events, 0.0 us)

commit v2 on v1

--- a/solution.py
+++ b/solution.py
@@ -102,32 +102,21 @@
     sizes,
     meta,
     fine,
-    mid,
-    coarse,
     neighbours,
     mask,
-    up_child_w,
-    up_parent_w,
-    up_out_w,
     up_bias,
     up_gain,
-    mid_child_w,
-    mid_parent_w,
-    mid_out_w,
     mid_bias,
     mid_gain,
-    same_self_w,
-    same_other_w,
-    same_out_w,
     same_bias,
     same_gain,
-    down_child_w,
-    down_parent_w,
-    down_out_w,
     down_bias,
-    down_gain,
-    mid_out,
-    coarse_out,
+    far,
+    down_hidden,
+    mid_new,
+    coarse_all_out,
+    near,
+    near_sem,
     fine_send,
     fine_got,
     fine_label_send,
@@ -145,15 +134,46 @@
     fine_row,
     fine_column,
     got_row,
-    got_column,
+    got_terms,
+    got_member,
     mid_terms,
     coarse_terms,
+    own_terms,
+    own_pick,
+    own_member,
+    in_terms,
+    in_pick,
+    in_member,
+    back_pick,
+    slot_rows,
+    slot_table,
+    slot_pick,
     fine_total,
     mid_total,
-    mid_new,
     send_sem,
     recv_sem,
 ):
+    (
+        mid,
+        up_parent_w,
+        up_child_w,
+        coarse,
+        mid_parent_w,
+        up_out_w,
+        mid_child_w,
+        down_child_w,
+        mid_out_w,
+        same_other_w,
+        same_self_w,
+        same_out_w,
+        down_parent_w,
+    ) = near
+    loads = [
+        pltpu.make_async_copy(source, target, near_sem.at[n])
+        for n, (source, target) in enumerate(zip(far, near))
+    ]
+    for load in loads:
+        load.start()
     groups, members, tile = sizes
     everyone = groups * members
     fine_count, width = fine.shape
@@ -164,7 +184,8 @@
     fine_blocks, mid_blocks = fine_count // LANES, mid_count // LANES
     fine_rows, mid_rows = round_up(fine_blocks, 8), round_up(mid_blocks, 8)
     chunk = coarse_count // groups
-    slots = neighbours.shape[1]
+    slots = neighbours.shape[0]
+    slot_base = round_up(slots, 8)
     g, d = lax.axis_index("grp"), lax.axis_index("dev")
     here = g * members + d
     ring = d * groups + g
@@ -209,10 +230,38 @@
         return copy
 
     fine_codes = meta[0:fine_rows, :]
+    fine_places = places(fine_codes)
+    fine_code_row = as_row(fine_codes, fine_blocks).astype(I32)
+    fine_place_row = as_row(fine_places, fine_blocks).astype(I32)
+    for c in range(4):
+        if fine_step > fine_cap:
+            low, high = c * fine_step + fine_cap, (c + 1) * fine_step
+            fine_got[low:high, :] = jnp.zeros((high - low, width), BF)
+        if mid_step > mid_cap:
+            low, high = c * mid_step + mid_cap, (c + 1) * mid_step
+            mid_got[low:high, :] = jnp.zeros((high - low, width), BF)
+    filled = (2 * groups + 1) * chunk
+    if rim.shape[0] > filled:
+        rim[filled:, :] = jnp.zeros((rim.shape[0] - filled, rim.shape[1]), BF)
+    fine_copies = [None] * 4
+    for n, c in enumerate((0, 3, 1, 2)):
+        wanted = jnp.where(fine_code_row == c + 1, fine_place_row, -1)
+        packed = dot(member_matrix(wanted, fine_cap), fine[...])
+        fine_send[c * fine_cap : (c + 1) * fine_cap, :] = packed.astype(BF)
+        if n == 0:
+            pl.semaphore_wait(barrier, len(greeted))
+        fine_copies[c] = start(
+            remote(
+                8 + c,
+                fine_send.at[c * fine_cap : (c + 1) * fine_cap],
+                fine_got.at[c * fine_step : c * fine_step + fine_cap],
+                along_all(OFFSETS[c]),
+            )
+        )
+
     fine_parents = meta[fine_rows : 2 * fine_rows, :]
     mid_codes = meta[2 * fine_rows : 2 * fine_rows + mid_rows, :]
     mid_parents = meta[2 * fine_rows + mid_rows : 2 * fine_rows + 2 * mid_rows, :]
-    fine_places = places(fine_codes)
     mid_places = places(mid_codes)
     fine_own = jnp.where(fine_codes == 0.0, fine_parents, -1.0)
     mid_own = jnp.where(mid_codes == 0.0, mid_parents, -1.0)
@@ -229,8 +278,6 @@
     mid_own_column = as_column(turned, at, mid_blocks)
     at += mid_rows
     mid_choice_column = as_column(turned, at, mid_blocks)
-    fine_code_row = as_row(fine_codes, fine_blocks).astype(I32)
-    fine_place_row = as_row(fine_places, fine_blocks).astype(I32)
     fine_own_row = as_row(fine_own, fine_blocks).astype(I32)
     for t in range(fine_count // tile):
         fine_row[t : t + 1, :] = fine_own_row[:, t * tile : (t + 1) * tile]
@@ -249,20 +296,7 @@
         as_row(mid_parents, mid_blocks).astype(I32),
         mid_place_column,
     )
-    for c in range(4):
-        if fine_step > fine_cap:
-            low, high = c * fine_step + fine_cap, (c + 1) * fine_step
-            fine_got[low:high, :] = jnp.zeros((high - low, width), BF)
-        if mid_step > mid_cap:
-            low, high = c * mid_step + mid_cap, (c + 1) * mid_step
-            mid_got[low:high, :] = jnp.zeros((high - low, width), BF)
-    filled = (2 * groups + 1) * chunk
-    if rim.shape[0] > filled:
-        rim[filled:, :] = jnp.zeros((rim.shape[0] - filled, rim.shape[1]), BF)
-
-    pl.semaphore_wait(barrier, len(greeted))
-
-    fine_copies, fine_label_copies, mid_label_copies = [None] * 4, [], []
+    fine_label_copies, mid_label_copies = [], []
     for c, offset in enumerate(OFFSETS):
         rows = slice(8 * c, 8 * c + 8)
         fine_label_copies.append(
@@ -271,18 +305,8 @@
         mid_label_copies.append(
             start(remote(4 + c, mid_label_send.at[rows], mid_label_got.at[rows], along_dev(offset)))
         )
-    for c in (0, 3, 1, 2):
-        wanted = jnp.where(fine_code_row == c + 1, fine_place_row, -1)
-        packed = dot(member_matrix(wanted, fine_cap), fine[...])
-        fine_send[c * fine_cap : (c + 1) * fine_cap, :] = packed.astype(BF)
-        fine_copies[c] = start(
-            remote(
-                8 + c,
-                fine_send.at[c * fine_cap : (c + 1) * fine_cap],
-                fine_got.at[c * fine_step : c * fine_step + fine_cap],
-                along_all(OFFSETS[c]),
-            )
-        )
+    for load in loads:
+        load.wait()
     mid_terms[...] = dot(mid[...], up_parent_w[...]).astype(BF)
     coarse_terms[...] = dot(coarse[...], mid_parent_w[...]).astype(BF)
 
@@ -302,6 +326,25 @@
         return carry
 
     lax.fori_loop(0, fine_count // tile, own_tile, 0)
+
+    own_pick[...] = pick_matrix(mid_own_column, coarse_count)
+    own_member[...] = member_matrix(mid_own_row, coarse_count)
+    back_pick[...] = pick_matrix(mid_choice_column, 4 * mid_cap)
+    own_terms[...] = dot(own_pick[...], coarse_terms[...]) + mid_bias[...]
+    mine = pl.ds(pl.multiple_of(g * chunk, chunk), chunk)
+    total_rows = members * coarse_count
+    local = neighbours[...] - (ring * chunk - groups * chunk)
+    local = jnp.where(local < 0, local + total_rows, local)
+    local = jnp.where(local >= total_rows, local - total_rows, local)
+    slot_rows[...] = jnp.zeros_like(slot_rows)
+    slot_rows[0:slots, :] = local.astype(F32)
+    slot_rows[slot_base : slot_base + slots, :] = mask[...].astype(F32)
+    slot_table[...] = slot_rows[...].T
+    slot_mine = slot_table[mine, :]
+    for k in range(slots):
+        slot_pick[k * chunk : (k + 1) * chunk, :] = pick_matrix(
+            slot_mine[:, k : k + 1].astype(I32), rim.shape[0]
+        )
 
     for copy in fine_label_copies + mid_label_copies:
         copy.wait_recv()
@@ -311,8 +354,6 @@
     per = fine_step // LANES
     for c in range(4):
         for s in range(per):
-            low = c * fine_step + s * LANES
-            got_column[low : low + LANES, :] = got_turned[:, 8 * c + s : 8 * c + s + 1]
             got_row[c : c + 1, s * LANES : (s + 1) * LANES] = fine_got_labels[
                 8 * c + s : 8 * c + s + 1, :
             ].astype(I32)
@@ -323,14 +364,22 @@
     mid_got_row = jnp.concatenate(
         [mid_got_labels[8 * c + s : 8 * c + s + 1, :] for c in range(4) for s in range(mid_per)], axis=1
     ).astype(I32)
+    for c in range(4):
+        part = slice(c * fine_step, (c + 1) * fine_step)
+        got_column = as_column(got_turned, 8 * c, per)
+        got_terms[part, :] = dot(pick_matrix(got_column, mid_count), mid_terms[...]).astype(BF)
+        got_member[:, part] = member_matrix(got_row[c : c + 1, :], mid_count)
+    in_pick[...] = pick_matrix(mid_got_column, coarse_count)
+    in_member[...] = member_matrix(mid_got_row, coarse_count)
+    in_terms[...] = dot(in_pick[...], coarse_terms[...]).astype(BF)
+
     for c in (1, 2, 0, 3):
         fine_copies[c].wait_recv()
-        low = c * fine_step
-        fine_total[...] += fine_part(
-            fine_got[low : low + fine_step, :],
-            got_column[low : low + fine_step, :],
-            got_row[c : c + 1, :],
-        )
+        part = slice(c * fine_step, (c + 1) * fine_step)
+        hidden = silu(
+            dot(fine_got[part, :], up_child_w[...]) + got_terms[part, :].astype(F32) + up_bias[...]
+        ).astype(BF)
+        fine_total[...] += dot(got_member[:, part], hidden)
     fine_sum = dot(fine_total[...].astype(BF), up_out_w[...])
     mid_new[...] = (mid[...].astype(F32) + layer_norm(fine_sum, up_gain[...])).astype(BF)
 
@@ -350,18 +399,16 @@
             )
         )
 
-    def mid_part(rows, column, row):
-        hidden = silu(
-            dot(rows, mid_child_w[...])
-            + dot(pick_matrix(column, coarse_count), coarse_terms[...])
-            + mid_bias[...]
-        ).astype(BF)
-        return dot(member_matrix(row, coarse_count), hidden)
-
-    mid_total[...] = mid_part(mid_new[...], mid_own_column, mid_own_row)
+    own_hidden = silu(dot(mid_new[...], mid_child_w[...]) + own_terms[...]).astype(BF)
+    mid_total[...] = dot(own_member[...], own_hidden)
+    child_terms = dot(mid_new[...], down_child_w[...]) + down_bias[...]
+    own_terms[...] = child_terms
     for copy in mid_copies:
         copy.wait_recv()
-    mid_total[...] += mid_part(mid_got[...], mid_got_column, mid_got_row)
+    in_hidden = silu(
+        dot(mid_got[...], mid_child_w[...]) + in_terms[...].astype(F32) + mid_bias[...]
+    ).astype(BF)
+    mid_total[...] += dot(in_member[...], in_hidden)
 
     sum_send[...] = mid_total[...].astype(BF)
     sum_copies = []
@@ -377,8 +424,6 @@
                 )
             )
         )
-    mine = pl.ds(pl.multiple_of(g * chunk, chunk), chunk)
-    child_terms = dot(mid_new[...], down_child_w[...]) + down_bias[...]
     hidden_sum = mid_total[mine, :]
     for k in range(1, groups):
         sum_copies[k - 1].wait_recv()
@@ -402,17 +447,17 @@
             )
         )
     self_terms = dot(coarse_new, same_self_w[...]) + same_bias[...]
-    total_rows = members * coarse_count
-    local = neighbours[mine, :] - (ring * chunk - groups * chunk)
-    local = jnp.where(local < 0, local + total_rows, local)
-    local = jnp.where(local >= total_rows, local - total_rows, local)
-    used = mask[mine, :].astype(F32)
+    used = slot_table[mine, :]
     for copy in rim_copies:
         copy.wait_recv()
     same_hidden = jnp.zeros((chunk, width), F32)
-    for k in range(slots):
-        picked = dot(pick_matrix(local[:, k : k + 1], rim.shape[0]), rim[...])
-        same_hidden += silu(self_terms + picked) * used[:, k : k + 1]
+    half = -(-slots // 2)
+    for low in range(0, slots, half):
+        high = min(low + half, slots)
+        picked = dot(slot_pick[low * chunk : high * chunk, :], rim[...])
+        for k in range(low, high):
+            terms = self_terms + picked[(k - low) * chunk : (k - low + 1) * chunk]
+            same_hidden += silu(terms) * used[:, slot_base + k : slot_base + k + 1]
     same_sum = dot(same_hidden.astype(BF), same_out_w[...])
     coarse_all[mine, :] = (
         coarse_new.astype(F32) + layer_norm(same_sum, same_gain[...])
@@ -425,9 +470,9 @@
         source = along_grp(-k)[0]
         theirs = pl.ds(pl.multiple_of(source * chunk, chunk), chunk)
         remote(first + k - 1, coarse_all.at[theirs], coarse_all.at[theirs], along_grp(-k)).wait_recv()
-    coarse_out[...] = coarse_all[...]
+    coarse_all_out[...] = coarse_all[...]
     down_terms = dot(coarse_all[...], down_parent_w[...]).astype(BF)
-    back_send[...] = dot(pick_matrix(mid_got_column, coarse_count), down_terms).astype(BF)
+    back_send[...] = dot(in_pick[...], down_terms).astype(BF)
     first += groups - 1
     back_copies = []
     for c, offset in enumerate(OFFSETS):
@@ -441,16 +486,21 @@
                 )
             )
         )
-    child_terms += dot(pick_matrix(mid_own_column, coarse_count), down_terms)
+    own_terms[...] += dot(own_pick[...], down_terms)
     for copy in back_copies:
         copy.wait_recv()
-    child_terms += dot(pick_matrix(mid_choice_column, 4 * mid_cap), back_got[...])
-    down_messages = dot(silu(child_terms).astype(BF), down_out_w[...])
+    child_terms = own_terms[...] + dot(back_pick[...], back_got[...])
+    down_hidden[...] = silu(child_terms).astype(BF)
+    for copy in started:
+        copy.wait_send()
+
+
+def finish(hidden, mid_new, coarse_all, down_out_w, down_gain, mid_out, coarse_out):
+    down_messages = dot(hidden[...], down_out_w[...])
     mid_out[...] = (
         mid_new[...].astype(F32) + layer_norm(down_messages, down_gain[...])
     ).astype(BF)
-    for copy in started:
-        copy.wait_send()
+    coarse_out[...] = coarse_all[...]
 
 
 def direction(owner, index, total):
@@ -501,17 +551,72 @@
     rim_rows = round_up((2 * groups + 1) * chunk, LANES)
     tile = 512 if fine_count % 512 == 0 else LANES
     copies = 16 + (groups - 1) + 2 * groups + (groups - 1) + 4
+    (
+        up_child_w,
+        up_parent_w,
+        up_out_w,
+        up_bias,
+        up_gain,
+        mid_child_w,
+        mid_parent_w,
+        mid_out_w,
+        mid_bias,
+        mid_gain,
+        same_self_w,
+        same_other_w,
+        same_out_w,
+        same_bias,
+        same_gain,
+        down_child_w,
+        down_parent_w,
+        down_out_w,
+        down_bias,
+        down_gain,
+    ) = weights
+    far = (
+        mid_nodes,
+        up_parent_w,
+        up_child_w,
+        coarse_nodes,
+        mid_parent_w,
+        up_out_w,
+        mid_child_w,
+        down_child_w,
+        mid_out_w,
+        same_other_w,
+        same_self_w,
+        same_out_w,
+        down_parent_w,
+    )
     vmem = pl.BlockSpec(memory_space=pltpu.VMEM)
-    operands = (meta, fine_nodes, mid_nodes, coarse_nodes, neighbours, neighbour_mask, *weights)
-    return pl.pallas_call(
+    hbm = pl.BlockSpec(memory_space=pl.ANY)
+    slots = neighbours.shape[1]
+    slot_size = round_up(2 * round_up(slots, 8), LANES)
+    operands = (
+        meta,
+        fine_nodes,
+        neighbours.T,
+        neighbour_mask.T,
+        up_bias,
+        up_gain,
+        mid_bias,
+        mid_gain,
+        same_bias,
+        same_gain,
+        down_bias,
+    )
+    down_hidden, mid_new, coarse_all = pl.pallas_call(
         functools.partial(kernel, (groups, members, tile)),
         out_shape=(
             jax.ShapeDtypeStruct((mid_count, width), BF),
+            jax.ShapeDtypeStruct((mid_count, width), BF),
             jax.ShapeDtypeStruct((coarse_count, width), BF),
         ),
-        in_specs=[vmem] * len(operands),
-        out_specs=(vmem, vmem),
+        in_specs=[vmem] * len(operands) + [(hbm,) * len(far)],
+        out_specs=(vmem, vmem, vmem),
         scratch_shapes=[
+            tuple(pltpu.VMEM(array.shape, BF) for array in far),
+            pltpu.SemaphoreType.DMA((len(far),)),
             pltpu.VMEM((4 * fine_cap, width), BF),
             pltpu.VMEM((4 * fine_step, width), BF),
             pltpu.VMEM((32, LANES), F32),
@@ -529,19 +634,38 @@
             pltpu.VMEM((fine_count // tile, tile), I32),
             pltpu.VMEM((fine_count, 1), I32),
             pltpu.VMEM((4, fine_step), I32),
-            pltpu.VMEM((4 * fine_step, 1), I32),
+            pltpu.VMEM((4 * fine_step, width), BF),
+            pltpu.VMEM((mid_count, 4 * fine_step), BF),
             pltpu.VMEM((mid_count, width), BF),
             pltpu.VMEM((coarse_count, width), BF),
             pltpu.VMEM((mid_count, width), F32),
+            pltpu.VMEM((mid_count, coarse_count), BF),
+            pltpu.VMEM((coarse_count, mid_count), BF),
+            pltpu.VMEM((4 * mid_step, width), BF),
+            pltpu.VMEM((4 * mid_step, coarse_count), BF),
+            pltpu.VMEM((coarse_count, 4 * mid_step), BF),
+            pltpu.VMEM((mid_count, 4 * mid_cap), BF),
+            pltpu.VMEM((slot_size, coarse_count), F32),
+            pltpu.VMEM((coarse_count, slot_size), F32),
+            pltpu.VMEM((slots * chunk, rim_rows), BF),
+            pltpu.VMEM((mid_count, width), F32),
             pltpu.VMEM((coarse_count, width), F32),
-            pltpu.VMEM((mid_count, width), BF),
             pltpu.SemaphoreType.DMA((copies,)),
             pltpu.SemaphoreType.DMA((copies,)),
         ],
         compiler_params=pltpu.CompilerParams(
-            collective_id=0, has_side_effects=True, vmem_limit_bytes=56 * 1024 * 1024
+            collective_id=0, has_side_effects=True, vmem_limit_bytes=60 * 1024 * 1024
         ),
-    )(*operands)
+    )(*operands, far)
+    return pl.pallas_call(
+        finish,
+        out_shape=(
+            jax.ShapeDtypeStruct((mid_count, width), BF),
+            jax.ShapeDtypeStruct((coarse_count, width), BF),
+        ),
+        in_specs=[vmem] * 5,
+        out_specs=(vmem, vmem),
+    )(down_hidden, mid_new, coarse_all, down_out_w, down_gain)
 
 
 def solution(mesh):

time: 104 us -> 99.8 us (0.960)
  local copies, waits for them, and re-layouts: 7.18 us -> 0 us
  Pallas kernels: 92.8 us -> 95.7 us
    unnamed x4 -> x0, local copies, waits for them, and re-layouts: 7.18 us -> none
    pallas_call x0 -> x1, Pallas kernels: none -> 3.5 us  [on_device(): pl.pallas_call(finish, out_shape=(jax.ShapeDtypeStruct((mid_count, width)...]
where the time goes in v2:
time: 99.8 us; the launch traced here: 99.2 us
  Pallas kernels  95.7 us (96%)
  other arithmetic  2.81 us (3%)
    pallas_call x1, Pallas kernels, on_device(): pl.pallas_call(functools.partial(kernel, (groups, members, tile)), out_sh...  92.2 us
    pallas_call x1, Pallas kernels, on_device(): pl.pallas_call(finish, out_shape=(jax.ShapeDtypeStruct((mid_count, width)...  3.5 us

profile of v2, /device:TPU:0, one launch (start us, length us, event | category | flops | bytes accessed | tf_op | source)
XLA Modules:
  0.0 99.2 jit_solution(2514460718158823684)
XLA Ops:
  0.6 0.7 subtract_reduce_fusion.1
  1.4 0.7 subtract_reduce_fusion
  2.1 1.3 %fusion.meta = f32[64,128]{1,0:T(8,128)} fusion(s32[5,128]{1,0:T(8,128)} %bitcast.23, s32[5,128]{1,0:T(8,128)S(1)} %select_select_fusion.1, s32[20,128]{1,0:T(8,128)} %bitcast.22, s32[20,128]{1,0:T(8,128)S(1)} %select_select_fusion), kind=kLoop, calls=%fused_computation.3 | loop fusion | flops 81920 | bytes 58368 | tf_op jit(solution)/shard_map/convert_element_type | solution.py:544
  3.5 92.2 %shard_map.284 = (bf16[640,512]{1,0:T(8,128)(2,1)}, bf16[640,512]{1,0:T(8,128)(2,1)}, bf16[640,512]{1,0:T(8,128)(2,1)}) custom-call(f32[64,128]{1,0:T(8,128)} %fusion.meta, bf16[2560,512]{1,0:T(8,128)(2,1)} %fine.1, s32[6,640]{1,0:T(8,128)} %bitcast.20, s32[6,640]{1,0:T(8,128)} %bitcast.21, f32[1,512]{1,0:T(1,128)} %bitcast.24, f32[1,512]{1,0:T(1,128)} %bitcast.25, ...), custom_call_target="tpu_custom_call" | custom-call | tf_op jit(solution)/shard_map/pallas_call | solution.py:608
  95.7 3.5 %shard_map.285 = (bf16[640,512]{1,0:T(8,128)(2,1)}, bf16[640,512]{1,0:T(8,128)(2,1)}) custom-call(bf16[640,512]{1,0:T(8,128)(2,1)} %get-tuple-element.5.hidden, bf16[640,512]{1,0:T(8,128)(2,1)} %get-tuple-element.6.mid_new, bf16[640,512]{1,0:T(8,128)(2,1)} %get-tuple-element.7.coarse_all, bf16[512,512]{1,0:T(8,128)(2,1)} %down_out_w.1, f32[1,512]{1,0:T(1,128)} %bitcast.31), custom_call_target="tpu_custom_call" | custom-call | tf_op jit(solution)/shard_map/pallas_call | solution.py:660
  (2 shorter events, 0.0 us)

commit v3 on v2

--- a/solution.py
+++ b/solution.py
@@ -200,14 +200,9 @@
     def along_grp(offset):
         return (lax.rem(g + offset + groups, groups), d)
 
-    def along_ring(offset):
-        to = lax.rem(ring + offset + everyone, everyone)
-        return (lax.rem(to, groups), lax.div(to, groups))
-
-    hops = [j for j in range(-groups, groups + 1) if j]
     greeted = [along_all(o) for o in OFFSETS]
     greeted += [along_dev(o) for o in OFFSETS]
-    greeted += [along_ring(j) for j in hops]
+    greeted += [along_grp(k) for k in range(1, groups)]
     barrier = pltpu.get_barrier_semaphore()
     for device in greeted:
         pl.semaphore_signal(barrier, inc=1, device_id=device, device_id_type=MESH)
@@ -408,23 +403,23 @@
     in_hidden = silu(
         dot(mid_got[...], mid_child_w[...]) + in_terms[...].astype(F32) + mid_bias[...]
     ).astype(BF)
-    mid_total[...] += dot(in_member[...], in_hidden)
-
-    sum_send[...] = mid_total[...].astype(BF)
+
     sum_copies = []
     for k in range(1, groups):
         to = along_grp(k)
+        theirs = pl.ds(pl.multiple_of(to[0] * chunk, chunk), chunk)
+        sum_send[theirs, :] = (mid_total[theirs, :] + dot(in_member[theirs, :], in_hidden)).astype(BF)
         sum_copies.append(
             start(
                 remote(
                     16 + k - 1,
-                    sum_send.at[pl.ds(pl.multiple_of(to[0] * chunk, chunk), chunk)],
+                    sum_send.at[theirs],
                     sum_got.at[(k - 1) * chunk : k * chunk],
                     to,
                 )
             )
         )
-    hidden_sum = mid_total[mine, :]
+    hidden_sum = mid_total[mine, :] + dot(in_member[mine, :], in_hidden)
     for k in range(1, groups):
         sum_copies[k - 1].wait_recv()
         hidden_sum += sum_got[(k - 1) * chunk : k * chunk, :].astype(F32)
@@ -434,20 +429,33 @@
     first = 16 + groups - 1
     own_rim = rim.at[groups * chunk : (groups + 1) * chunk]
     own_rim[...] = dot(coarse_new, same_other_w[...]).astype(BF)
-    rim_copies = []
-    for n, j in enumerate(hops):
+    rim_copies = [
+        start(remote(first, own_rim, rim.at[0:chunk], along_dev(1))),
+        start(remote(first + 1, own_rim, rim.at[2 * groups * chunk : filled], along_dev(-1))),
+    ]
+
+    def rim_part(place):
+        return rim.at[pl.ds(pl.multiple_of(place * chunk, chunk), chunk)]
+
+    for k in range(1, groups):
+        past = lax.div(g + k, groups)
+        start(remote(first + 1 + k, own_rim, rim_part(groups - k + groups * past), along_grp(k)))
+    self_terms = dot(coarse_new, same_self_w[...]) + same_bias[...]
+    used = slot_table[mine, :]
+    for k in range(1, groups):
+        past = 1 - lax.div(g - k + groups, groups)
+        held = rim_part(groups - k + groups * past)
+        remote(first + 1 + k, held, held, along_grp(-k)).wait_recv()
         rim_copies.append(
             start(
                 remote(
-                    first + n,
-                    own_rim,
-                    rim.at[(groups - j) * chunk : (groups - j + 1) * chunk],
-                    along_ring(j),
+                    first + groups + k,
+                    held,
+                    rim_part(2 * groups - k - groups * past),
+                    along_dev(2 * past - 1),
                 )
             )
         )
-    self_terms = dot(coarse_new, same_self_w[...]) + same_bias[...]
-    used = slot_table[mine, :]
     for copy in rim_copies:
         copy.wait_recv()
     same_hidden = jnp.zeros((chunk, width), F32)
@@ -463,7 +471,7 @@
         coarse_new.astype(F32) + layer_norm(same_sum, same_gain[...])
     ).astype(BF)
 
-    first += len(hops)
+    first += 2 * groups
     for k in range(1, groups):
         start(remote(first + k - 1, coarse_all.at[mine], coarse_all.at[mine], along_grp(k)))
     for k in range(1, groups):

time: 99.8 us -> 98.9 us (level)
  no operation moved by 1% of the time
where the time goes in v3:
time: 98.9 us; the launch traced here: 98.5 us
  Pallas kernels  95 us (96%)
  other arithmetic  2.81 us (3%)
    pallas_call x1, Pallas kernels, on_device(): pl.pallas_call(functools.partial(kernel, (groups, members, tile)), out_sh...  91.5 us
    pallas_call x1, Pallas kernels, on_device(): pl.pallas_call(finish, out_shape=(jax.ShapeDtypeStruct((mid_count, width)...  3.5 us

profile of v3, /device:TPU:0, one launch (start us, length us, event | category | flops | bytes accessed | tf_op | source)
XLA Modules:
  0.0 98.5 jit_solution(12107289833834762905)
XLA Ops:
  0.6 0.7 subtract_reduce_fusion.1
  1.4 0.7 subtract_reduce_fusion
  2.1 1.3 %fusion.meta = f32[64,128]{1,0:T(8,128)} fusion(s32[5,128]{1,0:T(8,128)} %bitcast.23, s32[5,128]{1,0:T(8,128)S(1)} %select_select_fusion.1, s32[20,128]{1,0:T(8,128)} %bitcast.22, s32[20,128]{1,0:T(8,128)S(1)} %select_select_fusion), kind=kLoop, calls=%fused_computation.3 | loop fusion | flops 81920 | bytes 58368 | tf_op jit(solution)/shard_map/convert_element_type | solution.py:552
  3.5 91.5 %shard_map.284 = (bf16[640,512]{1,0:T(8,128)(2,1)}, bf16[640,512]{1,0:T(8,128)(2,1)}, bf16[640,512]{1,0:T(8,128)(2,1)}) custom-call(f32[64,128]{1,0:T(8,128)} %fusion.meta, bf16[2560,512]{1,0:T(8,128)(2,1)} %fine.1, s32[6,640]{1,0:T(8,128)} %bitcast.20, s32[6,640]{1,0:T(8,128)} %bitcast.21, f32[1,512]{1,0:T(1,128)} %bitcast.24, f32[1,512]{1,0:T(1,128)} %bitcast.25, ...), custom_call_target="tpu_custom_call" | custom-call | tf_op jit(solution)/shard_map/pallas_call | solution.py:616
  95.0 3.5 %shard_map.285 = (bf16[640,512]{1,0:T(8,128)(2,1)}, bf16[640,512]{1,0:T(8,128)(2,1)}) custom-call(bf16[640,512]{1,0:T(8,128)(2,1)} %get-tuple-element.5.hidden, bf16[640,512]{1,0:T(8,128)(2,1)} %get-tuple-element.6.mid_new, bf16[640,512]{1,0:T(8,128)(2,1)} %get-tuple-element.7.coarse_all, bf16[512,512]{1,0:T(8,128)(2,1)} %down_out_w.1, f32[1,512]{1,0:T(1,128)} %bitcast.31), custom_call_target="tpu_custom_call" | custom-call | tf_op jit(solution)/shard_map/pallas_call | solution.py:668
  (2 shorter events, 0.0 us)
